TPU v7x, 32 devices: a whole 2x2x4 slice. The times are simulated.
32 devices in a mesh: dom: 8 (over z, x), band: 4 (over y, core).
Axes of the slice: x: 2, y: 2, z: 4, core: 2. Of those that a mesh axis runs over, the one named last changes fastest.
Arguments:
- states: float32 [160, 48, 3584], P('band', 'dom'), may hold values from -6 to 6
- potential: float32 [48, 3584], P('dom'), may hold values from -4 to 1
- counts: int32 [4], replicated, may hold values from 1 to 40, 128 in all
Outputs:
- filtered: float32 [160, 48, 3584], P('band', 'dom')
- projected: float32 [2, 160, 160], P(None, 'band', 'dom')
Inputs may be any that keep to these rules, and one draw needn't show every extreme that they name: The counts sum to 128; the largest equals 40.
All inputs are finite; a program needn't handle non-finite values.
Results may differ from a plain program's by a relative error of at most 0.000057.
Values sent between devices are 32-bit elements; how exact they have to be, the bound alone decides.
A program may use at most 128 MiB of HBM per device.

v0:
```python
import math

import jax
import jax.numpy as jnp
from jax import lax
from jax.sharding import PartitionSpec as P

NY = 56
NZ = 64


def padded_2(block, sides, width):
    for axis, dim in sides:
        count = lax.axis_size(axis)
        forward = [(i, i + 1) for i in range(count - 1)]
        backward = [(target, source) for source, target in forward]
        low = lax.ppermute(
            lax.slice_in_dim(block, block.shape[dim] - width, None, axis=dim), axis, forward
        )
        high = lax.ppermute(lax.slice_in_dim(block, 0, width, axis=dim), axis, backward)
        block = jnp.concatenate([low, block, high], axis=dim)
    return block


def stencil_weights():
    fact = math.factorial
    sides = [
        2.0 * (-1.0) ** (k + 1) * fact(6) ** 2 / (k * k * fact(6 - k) * fact(6 + k))
        for k in range(1, 7)
    ]
    return (-2.0 * sum(sides), sides)


def apply_hamiltonian(field, potential):
    center_weight, side_weights = stencil_weights()
    span_x, span_y, span_z = (field.shape[1], field.shape[2], field.shape[3])
    extended = padded_2(field, (("dom", 1),), 6)
    padded = jnp.pad(field, ((0, 0), (0, 0), (6, 6), (6, 6)))
    total = 3.0 * center_weight * field
    for step in range(1, 7):
        factor = side_weights[step - 1]
        near = extended[:, 6 + step : 6 + step + span_x]
        near = near + extended[:, 6 - step : 6 - step + span_x]
        near = near + padded[:, :, 6 + step : 6 + step + span_y, 6 : 6 + span_z]
        near = near + padded[:, :, 6 - step : 6 - step + span_y, 6 : 6 + span_z]
        near = near + padded[:, :, 6 : 6 + span_y, 6 + step : 6 + step + span_z]
        near = near + padded[:, :, 6 : 6 + span_y, 6 - step : 6 - step + span_z]
        total = total + factor * near
    return potential[None] * field - 0.5 * (1.0 / 0.36) * total


def contract_cells(left, right):
    return lax.dot_general(
        left,
        right,
        (((1,), (1,)), ((), ())),
        precision=lax.Precision.HIGHEST,
        preferred_element_type=jnp.float32,
    )


def local(states, potential, counts):
    capacity = states.shape[0]
    planes = states.shape[1]
    grid_states = states.reshape(capacity, planes, NY, NZ)
    grid_potential = potential.reshape(planes, NY, NZ)
    live_count = counts[lax.axis_index("band")]
    keep = (jnp.arange(capacity, dtype=jnp.int32) < live_count).astype(jnp.float32)
    start = grid_states * keep[:, None, None, None]
    first = (apply_hamiltonian(start, grid_potential) - 11.0 * start) / 11.0
    second = 2.0 * (apply_hamiltonian(first, grid_potential) - 11.0 * first) / 11.0 - start
    filtered = 2.0 * (apply_hamiltonian(second, grid_potential) - 11.0 * second) / 11.0 - first
    image = apply_hamiltonian(filtered, grid_potential)
    flat_states = filtered.reshape(capacity, -1)
    flat_image = image.reshape(capacity, -1)
    piece = lax.all_gather(flat_states, "band", axis=0, tiled=True)
    terms = jnp.stack([contract_cells(flat_states, piece), contract_cells(flat_image, piece)])
    projected = lax.psum_scatter(terms, "dom", scatter_dimension=2, tiled=True)
    return (filtered.reshape(capacity, planes, NY * NZ), projected)


def solution(mesh):
    return jax.shard_map(
        local,
        mesh=mesh,
        in_specs=(P("band", "dom", None), P("dom", None), P()),
        out_specs=(P("band", "dom", None), P(None, "band", "dom")),
        check_vma=False,
    )
```

profile of v0, /device:TPU:0, one launch (start us, length us, event | category | flops | bytes accessed | tf_op | source)
XLA Modules:
  0.0 1852.6 jit_solution(6906676464856110388)
XLA Ops:
  7.2 1.2 dynamic_slice.3
  8.5 0.6 compare_convert_fusion
  9.1 5.8 reshape.22
  14.9 6.3 copy_multiply_fusion
  21.2 1.3 collective-permute-start
  22.5 8.3 collective-permute-start.1
  30.9 143.6 %collective-permute-done = f32[40,6,56,64]{3,2,1,0:T(8,128)} collective-permute-done((f32[40,6,56,64]{3,2,1,0:T(8,128)}, f32[40,6,56,64]{3,2,1,0:T(8,128)}, u32[]{:S(2)}, u32[]{:S(2)}) %collective-permute-start) | collective-permute-done | bytes 3440672 | tf_op jit(solution)/shard_map/ppermute | solution.py:20
  174.5 147.6 %collective-permute-done.1 = f32[40,6,56,64]{3,2,1,0:T(8,128)} collective-permute-done((f32[40,6,56,64]{3,2,1,0:T(8,128)}, f32[40,6,56,64]{3,2,1,0:T(8,128)}, u32[]{:S(2)}, u32[]{:S(2)}) %collective-permute-start.1) | collective-permute-done | bytes 3440672 | tf_op jit(solution)/shard_map/ppermute | solution.py:17
  322.1 136.7 %broadcast_multiply_fusion = (f32[40,6,56,64]{3,2,1,0:T(8,128)}, f32[40,6,56,64]{3,2,1,0:T(8,128)S(1)}) fusion(f32[40,6,56,64]{3,2,1,0:T(8,128)} %copy_multiply_fusion, f32[40,6,56,64]{3,2,1,0:T(8,128)} %collective-permute-done, f32[40,6,56,64]{3,2,1,0:T(8,128)} %collective-permute-done.1, f32[6,56,64]{2,1,0:T(8,128)S(1)} %mul.149), kind=kLoop, calls=%fused_computation.380 | loop fusion | flops 50749440 | bytes 17289216 | tf_op jit(solution)/shard_map/div | solution.py:70
  458.8 1.3 collective-permute-start.2
  460.1 7.8 collective-permute-start.3
  467.9 143.9 %collective-permute-done.2 = f32[40,6,56,64]{3,2,1,0:T(8,128)} collective-permute-done((f32[40,6,56,64]{3,2,1,0:T(8,128)}, f32[40,6,56,64]{3,2,1,0:T(8,128)}, u32[]{:S(2)}, u32[]{:S(2)}) %collective-permute-start.2) | collective-permute-done | bytes 3440672 | tf_op jit(solution)/shard_map/ppermute | solution.py:20
  611.8 147.6 %collective-permute-done.3 = f32[40,6,56,64]{3,2,1,0:T(8,128)} collective-permute-done((f32[40,6,56,64]{3,2,1,0:T(8,128)}, f32[40,6,56,64]{3,2,1,0:T(8,128)}, u32[]{:S(2)}, u32[]{:S(2)}) %collective-permute-start.3) | collective-permute-done | bytes 3440672 | tf_op jit(solution)/shard_map/ppermute | solution.py:17
  759.4 136.7 %fusion.54 = f32[40,6,56,64]{3,2,1,0:T(8,128)} fusion(f32[40,6,56,64]{3,2,1,0:T(8,128)S(1)} %get-tuple-element.7, f32[40,6,56,64]{3,2,1,0:T(8,128)} %get-tuple-element.6, f32[40,6,56,64]{3,2,1,0:T(8,128)} %collective-permute-done.3, f32[40,6,56,64]{3,2,1,0:T(8,128)} %collective-permute-done.2, f32[6,56,64]{2,1,0:T(8,128)S(1)} %broadcast_multiply_fusion.1, ...), kind=kLoop, calls=%fused_computation.214 | loop fusion | flops 51609600 | bytes 20730016 | tf_op jit(solution)/shard_map/sub | solution.py:71
  896.1 1.3 collective-permute-start.4
  897.4 18.8 %collective-permute-start.5 = (f32[40,6,56,64]{3,2,1,0:T(8,128)}, f32[40,6,56,64]{3,2,1,0:T(8,128)}, u32[]{:S(2)}, u32[]{:S(2)}) collective-permute-start(f32[40,6,56,64]{3,2,1,0:T(8,128)} %fusion.54), channel_id=1, source_target_pairs={{0,4},{4,8},{8,12},{12,16},{16,20},{20,24},{24,28},{1,5},{5,9},{9,... | collective-permute-start | bytes 10321928 | tf_op jit(solution)/shard_map/ppermute | solution.py:17
  916.2 133.0 %collective-permute-done.4 = f32[40,6,56,64]{3,2,1,0:T(8,128)} collective-permute-done((f32[40,6,56,64]{3,2,1,0:T(8,128)}, f32[40,6,56,64]{3,2,1,0:T(8,128)}, u32[]{:S(2)}, u32[]{:S(2)}) %collective-permute-start.4) | collective-permute-done | bytes 3440672 | tf_op jit(solution)/shard_map/ppermute | solution.py:20
  1049.2 147.6 %collective-permute-done.5 = f32[40,6,56,64]{3,2,1,0:T(8,128)} collective-permute-done((f32[40,6,56,64]{3,2,1,0:T(8,128)}, f32[40,6,56,64]{3,2,1,0:T(8,128)}, u32[]{:S(2)}, u32[]{:S(2)}) %collective-permute-start.5) | collective-permute-done | bytes 3440672 | tf_op jit(solution)/shard_map/ppermute | solution.py:17
  1196.8 133.0 %fusion.95 = f32[40,6,56,64]{3,2,1,0:T(8,128)} fusion(f32[40,6,56,64]{3,2,1,0:T(8,128)} %fusion.54, f32[40,6,56,64]{3,2,1,0:T(8,128)} %collective-permute-done.5, f32[40,6,56,64]{3,2,1,0:T(8,128)} %collective-permute-done.4, f32[40,6,56,64]{3,2,1,0:T(8,128)S(1)} %get-tuple-element.7, f32[6,56,64]{2,1,0:T(8,128)S(1)} %mul.149), kind=kLoop, calls=%fused_computation.255 | loop fusion | flops 52469760 | bytes 17289216 | tf_op jit(solution)/shard_map/sub | solution.py:72
  1329.8 5.8 reshape.24
  1335.7 1.3 collective-permute-start.6
  1337.0 8.3 collective-permute-start.7
  1346.5 7.6 reshape.26
  1354.2 6.1 copy.12
  1360.2 128.5 %collective-permute-done.6 = f32[40,6,56,64]{3,2,1,0:T(8,128)} collective-permute-done((f32[40,6,56,64]{3,2,1,0:T(8,128)}, f32[40,6,56,64]{3,2,1,0:T(8,128)}, u32[]{:S(2)}, u32[]{:S(2)}) %collective-permute-start.6) | collective-permute-done | bytes 3440672 | tf_op jit(solution)/shard_map/ppermute | solution.py:20
  1488.7 147.6 %collective-permute-done.7 = f32[40,6,56,64]{3,2,1,0:T(8,128)} collective-permute-done((f32[40,6,56,64]{3,2,1,0:T(8,128)}, f32[40,6,56,64]{3,2,1,0:T(8,128)}, u32[]{:S(2)}, u32[]{:S(2)}) %collective-permute-start.7) | collective-permute-done | bytes 3440672 | tf_op jit(solution)/shard_map/ppermute | solution.py:17
  1636.3 135.9 %fusion.133 = f32[40,6,56,64]{3,2,1,0:T(8,128)} fusion(f32[40,6,56,64]{3,2,1,0:T(8,128)} %fusion.95, f32[40,6,56,64]{3,2,1,0:T(8,128)} %collective-permute-done.7, f32[40,6,56,64]{3,2,1,0:T(8,128)} %collective-permute-done.6, f32[6,56,64]{2,1,0:T(8,128)S(1)} %mul.149), kind=kLoop, calls=%fused_computation.293 | loop fusion | flops 48168960 | bytes 13848576 | tf_op jit(solution)/shard_map/sub | solution.py:49
  1772.2 6.0 reshape.25
  1778.2 16.1 convolution_bitcast_fusion.1
  1794.4 13.3 convolution_bitcast_fusion
  1807.8 37.3 %all-reduce.4 = f32[2,40,160]{1,0,2:T(2,128)S(1)} all-reduce(f32[2,40,160]{1,0,2:T(2,128)S(1)} %copy.11), channel_id=2, replica_groups=mesh['dom'=8,'band'=4] {'dom'}, use_global_device_ids=true, to_apply=%region_0.1.clone | all-reduce | flops 12800 | bytes 102400
  1845.1 0.6 constant_dynamic-slice_fusion
  (18 shorter events, 0.9 us)
Async XLA Ops:
  7.2 1771.0 %all-gather.2.cloned.1.call-start = ((), (), s32[]{:S(2)}) async-start(), calls=%async_computation | async-start | bytes 17203200 | tf_op jit(solution)/shard_map/all_gather | solution.py:76
  14.9 15.9 copy-start.3
  21.2 153.3 %collective-permute-start = (f32[40,6,56,64]{3,2,1,0:T(8,128)}, f32[40,6,56,64]{3,2,1,0:T(8,128)}, u32[]{:S(2)}, u32[]{:S(2)}) collective-permute-start(f32[40,6,56,64]{3,2,1,0:T(8,128)} %copy_multiply_fusion), channel_id=1, source_target_pairs={{4,0},{8,4},{12,8},{16,12},{20,16},{24,20},{28,24},{5,1},{9,5},{13... | collective-permute-start | bytes 10321928 | tf_op jit(solution)/shard_map/ppermute | solution.py:20
  22.5 299.6 %collective-permute-start.1 = (f32[40,6,56,64]{3,2,1,0:T(8,128)}, f32[40,6,56,64]{3,2,1,0:T(8,128)}, u32[]{:S(2)}, u32[]{:S(2)}) collective-permute-start(f32[40,6,56,64]{3,2,1,0:T(8,128)} %copy_multiply_fusion), channel_id=1, source_target_pairs={{0,4},{4,8},{8,12},{12,16},{16,20},{20,24},{24,28},{1,5},{5,9},{9,... | collective-permute-start | bytes 10321928 | tf_op jit(solution)/shard_map/ppermute | solution.py:17
  458.8 153.0 %collective-permute-start.2 = (f32[40,6,56,64]{3,2,1,0:T(8,128)}, f32[40,6,56,64]{3,2,1,0:T(8,128)}, u32[]{:S(2)}, u32[]{:S(2)}) collective-permute-start(f32[40,6,56,64]{3,2,1,0:T(8,128)} %get-tuple-element.6), channel_id=1, source_target_pairs={{4,0},{8,4},{12,8},{16,12},{20,16},{24,20},{28,24},{5,1},{9,5},{13... | collective-permute-start | bytes 10321928 | tf_op jit(solution)/shard_map/ppermute | solution.py:20
  460.1 299.3 %collective-permute-start.3 = (f32[40,6,56,64]{3,2,1,0:T(8,128)}, f32[40,6,56,64]{3,2,1,0:T(8,128)}, u32[]{:S(2)}, u32[]{:S(2)}) collective-permute-start(f32[40,6,56,64]{3,2,1,0:T(8,128)} %get-tuple-element.6), channel_id=1, source_target_pairs={{0,4},{4,8},{8,12},{12,16},{16,20},{20,24},{24,28},{1,5},{5,9},{9,... | collective-permute-start | bytes 10321928 | tf_op jit(solution)/shard_map/ppermute | solution.py:17
  896.1 153.0 %collective-permute-start.4 = (f32[40,6,56,64]{3,2,1,0:T(8,128)}, f32[40,6,56,64]{3,2,1,0:T(8,128)}, u32[]{:S(2)}, u32[]{:S(2)}) collective-permute-start(f32[40,6,56,64]{3,2,1,0:T(8,128)} %fusion.54), channel_id=1, source_target_pairs={{4,0},{8,4},{12,8},{16,12},{20,16},{24,20},{28,24},{5,1},{9,5},{13... | collective-permute-start | bytes 10321928 | tf_op jit(solution)/shard_map/ppermute | solution.py:20
  897.4 299.4 %collective-permute-start.5 = (f32[40,6,56,64]{3,2,1,0:T(8,128)}, f32[40,6,56,64]{3,2,1,0:T(8,128)}, u32[]{:S(2)}, u32[]{:S(2)}) collective-permute-start(f32[40,6,56,64]{3,2,1,0:T(8,128)} %fusion.54), channel_id=1, source_target_pairs={{0,4},{4,8},{8,12},{12,16},{16,20},{20,24},{24,28},{1,5},{5,9},{9,... | collective-permute-start | bytes 10321928 | tf_op jit(solution)/shard_map/ppermute | solution.py:17
  1329.8 15.5 copy-start.4
  1335.7 153.0 %collective-permute-start.6 = (f32[40,6,56,64]{3,2,1,0:T(8,128)}, f32[40,6,56,64]{3,2,1,0:T(8,128)}, u32[]{:S(2)}, u32[]{:S(2)}) collective-permute-start(f32[40,6,56,64]{3,2,1,0:T(8,128)} %fusion.95), channel_id=1, source_target_pairs={{4,0},{8,4},{12,8},{16,12},{20,16},{24,20},{28,24},{5,1},{9,5},{13... | collective-permute-start | bytes 10321928 | tf_op jit(solution)/shard_map/ppermute | solution.py:20
  1337.0 299.4 %collective-permute-start.7 = (f32[40,6,56,64]{3,2,1,0:T(8,128)}, f32[40,6,56,64]{3,2,1,0:T(8,128)}, u32[]{:S(2)}, u32[]{:S(2)}) collective-permute-start(f32[40,6,56,64]{3,2,1,0:T(8,128)} %fusion.95), channel_id=1, source_target_pairs={{0,4},{4,8},{8,12},{12,16},{16,20},{20,24},{24,28},{1,5},{5,9},{9,... | collective-permute-start | bytes 10321928 | tf_op jit(solution)/shard_map/ppermute | solution.py:17
  1772.2 6.0 copy-start.1
  1778.2 16.2 copy-start
  1778.2 16.2 copy-start.2
Sparse Core Ops, SparseCore 0:
  1335.8 90.0 all-gather.1
where the time goes:
time: 1860 us; the launch traced here: 1850 us
  waiting for transfers between devices  1140 us (61%)
  other arithmetic  549 us (30%)
  starting transfers between devices  48.4 us (3%)
  blocking collectives  37.3 us (2%)
  local copies, waits for them, and re-layouts  34 us (2%)
  matrix products  29.4 us (2%)
    ppermute x4, waiting for transfers between devices, padded_2(): lax.ppermute(lax.slice_in_dim(block, block.shape[dim] - width, None, axis...  590 us
    ppermute x4, waiting for transfers between devices, padded_2(): lax.ppermute(lax.slice_in_dim(block, 0, width, axis=dim), axis, backward)  549 us
    sub x1, other arithmetic, local(): 2.0 * (apply_hamiltonian(first, grid_potential) - 11.0 * first) / 11.0  137 us
    div x1, other arithmetic, local(): first = (apply_hamiltonian(start, grid_potential) - 11.0 * start) / 11.0  137 us
    sub x1, other arithmetic, apply_hamiltonian(): return potential[None] * field - 0.5 * (1.0 / 0.36) * total  136 us
    sub x1, other arithmetic, local(): 2.0 * (apply_hamiltonian(second, grid_potential) - 11.0 * second) / 11.0  133 us
    ppermute x4, starting transfers between devices, padded_2(): lax.ppermute(lax.slice_in_dim(block, block.shape[dim] - width, None, axis...  43.2 us
    unnamed x1, blocking collectives  37.3 us
  transfers between devices with their start and end apart: 9, of which 8 were waited for; matrix products, arithmetic and copies ran while one was open for 8% of the time, Pallas kernels for 0%

commit v1 on v0

v1 whole, which is shorter than its diff:
```python
import functools
import math

import jax
import jax.numpy as jnp
import ml_dtypes
import numpy as np
from jax import lax
from jax.experimental import pallas as pl
from jax.experimental.pallas import tpu as pltpu
from jax.sharding import PartitionSpec as P

NY = 56
NZ = 64
REACH = 6
LANES = 256
EDGE = REACH * NZ
VMEM_BYTES = 60 * 1024 * 1024


def stencil_weights():
    fact = math.factorial
    sides = [
        2.0 * (-1.0) ** (k + 1) * fact(6) ** 2 / (k * k * fact(6 - k) * fact(6 + k))
        for k in range(1, 7)
    ]
    return (-2.0 * sum(sides), sides)


CENTER, SIDES = stencil_weights()
SCALE = -0.5 * (1.0 / 0.36)


def side_table(distance):
    table = np.zeros(distance.shape, np.float64)
    for step in range(1, REACH + 1):
        table += np.where(np.abs(distance) == step, SCALE * SIDES[step - 1], 0.0)
    return table


def halves(table):
    high = table.astype(ml_dtypes.bfloat16)
    low = (table - high.astype(np.float64)).astype(ml_dtypes.bfloat16)
    return np.stack([high, low])


def plane_matrix():
    k = np.arange(LANES + 2 * EDGE)[:, None] - EDGE
    n = np.arange(LANES)[None, :]
    dy = k // NZ - n // NZ
    dz = k % NZ - n % NZ
    return halves(np.where(dz == 0, side_table(dy), 0.0) + np.where(dy == 0, side_table(dz), 0.0))


def row_table(parts, each, planes, rows):
    r = np.arange(parts * rows)
    source, inner = r // rows, r % rows
    valid = inner < each * planes
    slot = np.where(valid, inner // planes, -1)
    return source, slot, inner % planes, valid


def cross_matrix(parts, each, planes, rows):
    source, slot, plane, valid = row_table(parts, each, planes, rows)
    x = source * planes + plane
    same = (slot[:, None] == slot[None, :]) & valid[:, None] & valid[None, :]
    return halves(np.where(same, side_table(x[:, None] - x[None, :]), 0.0))


def spread_matrix(parts, each, planes, rows):
    source, slot, plane, valid = row_table(parts, each, planes, rows)
    x = source * planes + plane
    return ((x[:, None] == np.arange(parts * planes)[None, :]) & valid[:, None]).astype(np.float32)


def split(value):
    high = value.astype(jnp.bfloat16)
    return high, (value - high.astype(jnp.float32)).astype(jnp.bfloat16)


def dot3(left_high, left_low, right_high, right_low):
    dot = functools.partial(jnp.dot, preferred_element_type=jnp.float32)
    return dot(left_high, right_high) + (dot(left_high, right_low) + dot(left_low, right_high))


def filter_kernel(start, potential, spread, near, cross, filtered, image, field, held, first, second):
    cells = start.shape[1]
    chunks = cells // LANES
    rows = start.shape[0]
    for part in range(2):
        for half in range(2):
            held[part, half, :, 0:EDGE] = jnp.zeros((rows, EDGE), jnp.bfloat16)
            held[part, half, :, EDGE + cells :] = jnp.zeros((rows, EDGE), jnp.bfloat16)

    def keep(part, c, value):
        at = pl.ds(pl.multiple_of(c * LANES + EDGE, 128), LANES)
        high, low = split(value)
        held[part, 0, :, at] = high
        held[part, 1, :, at] = low

    @pl.loop(0, chunks)
    def _(c):
        at = pl.ds(pl.multiple_of(c * LANES, 128), LANES)
        field[:, at] = jnp.dot(
            spread[...], potential[:, at], precision=lax.Precision.HIGHEST, preferred_element_type=jnp.float32
        ) + 3.0 * CENTER * SCALE
        keep(0, c, start[:, at])

    def apply(part, now, before, out, gain, own, last):
        @pl.loop(0, chunks)
        def _(c):
            at = pl.ds(pl.multiple_of(c * LANES, 128), LANES)
            wide = pl.ds(pl.multiple_of(c * LANES, 128), LANES + 2 * EDGE)
            mid = pl.ds(pl.multiple_of(c * LANES + EDGE, 128), LANES)
            total = dot3(held[part, 0, :, wide], held[part, 1, :, wide], near[0], near[1])
            total += dot3(cross[0], cross[1], held[part, 0, :, mid], held[part, 1, :, mid])
            value = now[:, at]
            result = gain * (field[:, at] * value + total) + own * value
            if before is not None:
                result = result - before[:, at]
            out[:, at] = result
            if not last:
                keep(1 - part, c, result)

    apply(0, start, None, first, 1.0 / 11.0, -1.0, False)
    apply(1, first, start, second, 2.0 / 11.0, -2.0, False)
    apply(0, second, first, filtered, 2.0 / 11.0, -2.0, False)
    apply(1, filtered, None, image, 1.0, 0.0, True)


def run_filter(start, potential, parts, each, planes, rows):
    total, cells = start.shape
    spread = jnp.asarray(spread_matrix(parts, each, planes, rows))
    near = jnp.asarray(plane_matrix())
    cross = jnp.asarray(cross_matrix(parts, each, planes, rows))
    shape = jax.ShapeDtypeStruct((total, cells), jnp.float32)
    work = pltpu.VMEM((total, cells), jnp.float32)
    return pl.pallas_call(
        filter_kernel,
        out_shape=(shape, shape),
        in_specs=[pl.BlockSpec(memory_space=pltpu.VMEM)] * 5,
        out_specs=(pl.BlockSpec(memory_space=pltpu.VMEM),) * 2,
        scratch_shapes=[work, pltpu.VMEM((2, 2, total, cells + 2 * EDGE), jnp.bfloat16), work, work],
        compiler_params=pltpu.CompilerParams(vmem_limit_bytes=VMEM_BYTES),
        name="filter_states",
    )(start, potential, spread, near, cross)


def gram_kernel(own, image, every, same, fold_left, fold_right, out, total):
    step = pl.program_id(0)

    @pl.when(step == 0)
    def _():
        total[...] = jnp.zeros_like(total)

    every_high, every_low = split(every[...])
    dot = functools.partial(
        lax.dot_general, dimension_numbers=(((1,), (1,)), ((), ())), preferred_element_type=jnp.float32
    )
    for which, ref in enumerate((own, image)):
        high, low = split(ref[...])
        total[which] += dot(high, every_high) + (dot(high, every_low) + dot(low, every_high))

    @pl.when(step == pl.num_programs(0) - 1)
    def _():
        exact = functools.partial(
            jnp.dot, precision=lax.Precision.HIGHEST, preferred_element_type=jnp.float32
        )
        for which in range(2):
            out[which] = exact(exact(fold_left[...], total[which] * same[...]), fold_right[...])


def run_gram(own, image, every, parts, each, planes, rows, capacity, bands):
    total, cells = own.shape
    width = every.shape[0]
    source, slot, plane, valid = row_table(parts, each, planes, rows)
    index = source * each + slot
    fold = ((index[None, :] == np.arange(capacity)[:, None]) & valid[None, :]).astype(np.float32)
    plane = np.where(valid, plane, -1)
    same = (plane[:, None] == np.tile(plane, bands)[None, :]).astype(np.float32)
    fold_right = np.kron(np.eye(bands, dtype=np.float32), fold.T)
    block = pl.BlockSpec((total, LANES), lambda i: (0, i))
    return pl.pallas_call(
        gram_kernel,
        grid=(cells // LANES,),
        out_shape=jax.ShapeDtypeStruct((2, capacity, bands * capacity), jnp.float32),
        in_specs=[
            block,
            block,
            pl.BlockSpec((width, LANES), lambda i: (0, i)),
            pl.BlockSpec(memory_space=pltpu.VMEM),
            pl.BlockSpec(memory_space=pltpu.VMEM),
            pl.BlockSpec(memory_space=pltpu.VMEM),
        ],
        out_specs=pl.BlockSpec((2, capacity, bands * capacity), lambda i: (0, 0, 0)),
        scratch_shapes=[pltpu.VMEM((2, total, width), jnp.float32)],
        compiler_params=pltpu.CompilerParams(vmem_limit_bytes=VMEM_BYTES),
        name="gram",
    )(own, image, every, jnp.asarray(same), jnp.asarray(fold), jnp.asarray(fold_right))


def local(states, potential, counts):
    capacity, planes, cells = states.shape
    parts, bands = lax.axis_size("dom"), lax.axis_size("band")
    each = -(-capacity // parts)
    rows = -(-each * planes // 8) * 8
    live_count = counts[lax.axis_index("band")]
    keep = (jnp.arange(capacity, dtype=jnp.int32) < live_count).astype(jnp.float32)
    start = states * keep[:, None, None]
    start = jnp.pad(start, ((0, parts * each - capacity), (0, 0), (0, 0)))
    start = start.reshape(parts, each * planes, cells)
    start = jnp.pad(start, ((0, 0), (0, rows - each * planes), (0, 0)))
    whole_potential = lax.all_gather(potential, "dom", axis=0, tiled=True)
    start = lax.all_to_all(start, "dom", 0, 0, tiled=True).reshape(parts * rows, cells)
    filtered, image = run_filter(start, whole_potential, parts, each, planes, rows)
    back = lambda a: lax.all_to_all(a.reshape(parts, rows, cells), "dom", 0, 0, tiled=True).reshape(parts * rows, cells)
    filtered = back(filtered)
    every = lax.all_gather(filtered, "band", axis=0, tiled=True)
    image = back(image)
    terms = run_gram(filtered, image, every, parts, each, planes, rows, capacity, bands)
    projected = lax.psum_scatter(terms, "dom", scatter_dimension=2, tiled=True)
    result = filtered.reshape(parts, rows, cells)[:, : each * planes]
    result = result.reshape(parts * each, planes, cells)[:capacity]
    return result, projected


def solution(mesh):
    return jax.shard_map(
        local,
        mesh=mesh,
        in_specs=(P("band", "dom", None), P("dom", None), P()),
        out_specs=(P("band", "dom", None), P(None, "band", "dom")),
        check_vma=False,
    )
```

time: 1860 us -> 434 us (0.23)
  waiting for transfers between devices: 1140 us -> 75.3 us
  other arithmetic: 549 us -> 3.07 us
  blocking collectives: 37.3 us -> 226 us
  Pallas kernels: 0 us -> 72.1 us
  starting transfers between devices: 48.4 us -> 12.1 us
  matrix products: 29.4 us -> 0 us
    ppermute x8 -> x0, waiting for transfers between devices: 1140 us -> none  [the longest x4 590 us: padded_2(): lax.ppermute(lax.slice_in_dim(block, block.shape[dim] - width, None, axis...]
    sub x3 -> x0, other arithmetic: 406 us -> none  [the longest x1 137 us: local(): 2.0 * (apply_hamiltonian(first, grid_potential) - 11.0 * first) / 11.0]
    div x1 -> x0, other arithmetic: 137 us -> none  [local(): first = (apply_hamiltonian(start, grid_potential) - 11.0 * start) / 11.0]
    all_gather x0 -> x1, blocking collectives: none -> 104 us  [local(): whole_potential = lax.all_gather(potential, 'dom', axis=0, tiled=True)]
    all_to_all x0 -> x1, blocking collectives: none -> 83.1 us  [local(): lax.all_to_all(a.reshape(parts, rows, cells), 'dom', 0, 0, tiled=True)]
    pallas_call x0 -> x2, Pallas kernels: none -> 72.1 us  [the longest x1 50.1 us: run_filter(): pl.pallas_call(filter_kernel, out_shape=(shape, shape), in_specs=[pl.Bloc...]
    all_to_all x0 -> x2, waiting for transfers between devices: none -> 66.8 us  [the longest x1 66.8 us: local(): lax.all_to_all(a.reshape(parts, rows, cells), 'dom', 0, 0, tiled=True)]
    ppermute x8 -> x0, starting transfers between devices: 48.3 us -> none  [the longest x4 43.2 us: padded_2(): lax.ppermute(lax.slice_in_dim(block, block.shape[dim] - width, None, axis...]
  transfers between devices with their start and end apart: 9 -> 3, of which waited for: 8 -> 2; matrix products, arithmetic and copies ran while one was open for 8% -> 3% of each run, Pallas kernels for 0% -> 0%
where the time goes in v1:
time: 434 us; the launch traced here: 433 us
  blocking collectives  226 us (52%)
  waiting for transfers between devices  75.3 us (17%)
  Pallas kernels  72.1 us (17%)
  local copies, waits for them, and re-layouts  29.7 us (7%)
  between operations  14.8 us (3%)
  starting transfers between devices  12.1 us (3%)
    all_gather x1, blocking collectives, local(): whole_potential = lax.all_gather(potential, 'dom', axis=0, tiled=True)  104 us
    all_to_all x1, blocking collectives, local(): lax.all_to_all(a.reshape(parts, rows, cells), 'dom', 0, 0, tiled=True)  83.1 us
    all_to_all x1, waiting for transfers between devices, local(): lax.all_to_all(a.reshape(parts, rows, cells), 'dom', 0, 0, tiled=True)  66.8 us
    pallas_call x1, Pallas kernels, run_filter(): pl.pallas_call(filter_kernel, out_shape=(shape, shape), in_specs=[pl.Bloc...  50.1 us
    unnamed x1, blocking collectives  38.8 us
    pallas_call x1, Pallas kernels, run_gram(): pl.pallas_call(gram_kernel, grid=(cells // LANES,), out_shape=jax.ShapeDt...  22 us
    unnamed x8, local copies, waits for them, and re-layouts  9.1 us
  transfers between devices with their start and end apart: 3, of which 2 were waited for; matrix products, arithmetic and copies ran while one was open for 3% of the time, Pallas kernels for 0%

profile of v1, /device:TPU:0, one launch (start us, length us, event | category | flops | bytes accessed | tf_op | source)
XLA Modules:
  0.0 433.1 jit_solution(9664504529662459760)
XLA Ops:
  7.2 1.2 dynamic_slice.3
  8.4 0.6 compare_convert_fusion
  9.1 2.4 broadcast_multiply_fusion
  11.5 4.2 copy.15
  15.6 4.9 %reshape.30 = f32[8,30,3584]{2,1,0:T(8,128)} reshape(f32[40,6,3584]{2,1,0:T(8,128)} %copy.15) | data formatting | bytes 6881280 | tf_op jit(solution)/shard_map/reshape | solution.py:211
  20.5 4.3 pad.4
  24.8 0.0 copy-start
  24.8 7.4 %all-to-all-start = ((f32[8,32,3584]{2,1,0:T(8,128)}), f32[8,32,3584]{2,1,0:T(8,128)}, u32[]{:S(2)}, u32[]{:S(2)}) async-start(f32[8,32,3584]{2,1,0:T(8,128)} %pad.4), calls=%async_computation | async-start | bytes 7340032 | tf_op jit(solution)/shard_map/all_to_all | solution.py:214
  32.2 0.0 all-gather.3.cloned.1.call-start
  32.2 0.0 copy-done
  32.2 104.1 %all-gather = f32[8,6,3584]{2,1,0:T(8,128)S(1)} all-gather(f32[1,6,3584]{2,1,0:T(8,128)S(1)} %bitcast.14), channel_id=1, replica_groups=mesh['dom'=8,'band'=4] {'dom'}, dimensions={0}, use_global_device_ids=true | all-gather | bytes 774144 | tf_op jit(solution)/shard_map/all_gather | solution.py:213
  136.4 0.9 reshape.38.potential
  137.3 0.0 all-to-all-done
  137.3 50.1 %filter_states.1 = (f32[256,3584]{1,0:T(8,128)}, f32[256,3584]{1,0:T(8,128)}) custom-call(f32[256,3584]{1,0:T(8,128)} %bitcast.1.start, f32[48,3584]{1,0:T(8,128)} %reshape.38.potential, f32[256,48]{1,0:T(8,128)} %constant.22.clone.spread, bf16[2,1024,256]{2,1,0:T(8,128)(2,1)} %constant.23.clone.near, bf16[2,256,256]{2,1,0:T(8,128)(2,1)} %constant.24.clone.cross), custom_call_target="tpu_custom_call" | custom-call | tf_op jit(solution)/shard_map/filter_states/pallas_call | solution.py:138
  187.4 83.1 %all_to_all.15 = f32[8,32,3584]{2,1,0:T(8,128)} all-to-all(f32[8,32,3584]{2,1,0:T(8,128)} %bitcast.13), channel_id=1, replica_groups=mesh['dom'=8,'band'=4] {'dom'}, dimensions={0} | all-to-all | bytes 7340032 | tf_op jit(solution)/shard_map/all_to_all | solution.py:216
  270.5 0.0 all-gather.3.cloned.1.call-update
  270.6 0.0 copy-start.1
  270.6 4.7 %all-to-all-start.2 = ((f32[8,32,3584]{2,1,0:T(8,128)}), f32[8,32,3584]{2,1,0:T(8,128)}, u32[]{:S(2)}, u32[]{:S(2)}) async-start(f32[8,32,3584]{2,1,0:T(8,128)} %bitcast.12), calls=%async_computation.2 | async-start | bytes 7340032 | tf_op jit(solution)/shard_map/all_to_all | solution.py:216
  275.3 0.0 copy-done.1
  275.3 0.6 dynamic-slice
  276.5 5.0 %reshape.33 = f32[40,6,3584]{2,1,0:T(8,128)} reshape(f32[8,30,3584]{2,1,0:T(8,128)} %bitcast.10) | data formatting | bytes 6881280 | tf_op jit(solution)/shard_map/reshape | solution.py:223
  281.5 6.9 %copy.17 = f32[40,6,3584]{2,0,1:T(8,128)} copy(f32[40,6,3584]{2,1,0:T(8,128)} %reshape.33) | data formatting | bytes 6881280
  288.5 66.8 %all-to-all-done.2 = f32[8,32,3584]{2,1,0:T(8,128)} async-done(((f32[8,32,3584]{2,1,0:T(8,128)}), f32[8,32,3584]{2,1,0:T(8,128)}, u32[]{:S(2)}, u32[]{:S(2)}) %all-to-all-start.2) | async-done | bytes 3670048 | tf_op jit(solution)/shard_map/all_to_all | solution.py:216
  355.2 8.5 %all-gather.3.cloned.1.call-done.every = f32[1024,3584]{1,0:T(8,128)} async-done(((f32[256,3584]{1,0:T(8,128)}), f32[1024,3584]{1,0:T(8,128)}) %all-gather.3.cloned.1.call-update) | async-done | bytes 14680080 | tf_op jit(solution)/shard_map/all_gather | solution.py:218
  363.8 22.0 %gram.1 = f32[2,40,160]{2,1,0:T(8,128)} custom-call(f32[256,3584]{1,0:T(8,128)} %bitcast.11, f32[256,3584]{1,0:T(8,128)} %bitcast.6.image, f32[1024,3584]{1,0:T(8,128)} %all-gather.3.cloned.1.call-done.every, f32[256,1024]{1,0:T(8,128)} %constant.25.clone.same, f32[40,256]{1,0:T(8,128)} %constant.26.clone.fold_left, f32[1024,160]{1,0:T(8,128)} %constant.27.clone.fold_right), custom_call_target="tpu_custom_call" | custom-call | tf_op jit(solution)/shard_map/gram/pallas_call | solution.py:183
  385.8 1.0 copy.16
  386.8 38.8 %all-reduce.1 = f32[2,40,160]{1,0,2:T(2,128)S(1)} all-reduce(f32[2,40,160]{1,0,2:T(2,128)S(1)} %copy.16), channel_id=2, replica_groups=mesh['dom'=8,'band'=4] {'dom'}, use_global_device_ids=true, to_apply=%region_0.1.clone | all-reduce | flops 12800 | bytes 102400
  425.6 0.6 constant_dynamic-slice_fusion
Async XLA Ops:
  24.8 7.4 %copy-start = (f32[6,3584]{1,0:T(8,128)S(1)}, f32[6,3584]{1,0:T(8,128)}, u32[]{:S(2)}) copy-start(f32[6,3584]{1,0:T(8,128)} %param.10) | copy-start | bytes 258052
  24.8 112.5 %all-to-all-start = ((f32[8,32,3584]{2,1,0:T(8,128)}), f32[8,32,3584]{2,1,0:T(8,128)}, u32[]{:S(2)}, u32[]{:S(2)}) async-start(f32[8,32,3584]{2,1,0:T(8,128)} %pad.4), calls=%async_computation | async-start | bytes 7340032 | tf_op jit(solution)/shard_map/all_to_all | solution.py:214
  32.2 331.6 %all-gather.3.cloned.1.call-start = ((), (), s32[]{:S(2)}) async-start(), calls=%async_computation.3 | async-start | bytes 18350080 | tf_op jit(solution)/shard_map/all_gather | solution.py:218
  270.6 4.7 %copy-start.1 = (u32[32]{0:T(128)S(1)}, u32[32]{0:T(128)}, u32[]{:S(2)}) copy-start(u32[32]{0:T(128)} %constant.34) | copy-start | bytes 388
  270.6 84.7 %all-to-all-start.2 = ((f32[8,32,3584]{2,1,0:T(8,128)}), f32[8,32,3584]{2,1,0:T(8,128)}, u32[]{:S(2)}, u32[]{:S(2)}) async-start(f32[8,32,3584]{2,1,0:T(8,128)} %bitcast.12), calls=%async_computation.2 | async-start | bytes 7340032 | tf_op jit(solution)/shard_map/all_to_all | solution.py:216
Sparse Core Ops, SparseCore 0:
  270.7 93.0 all-gather.2

commit v2 on v1

v2 whole, which is shorter than its diff:
```python
import functools
import math

import jax
import jax.numpy as jnp
import ml_dtypes
import numpy as np
from jax import lax
from jax.experimental import pallas as pl
from jax.experimental.pallas import tpu as pltpu
from jax.sharding import PartitionSpec as P

NY = 56
NZ = 64
REACH = 6
LANES = 256
EDGE = REACH * NZ
VMEM_BYTES = 62 * 1024 * 1024


def stencil_weights():
    fact = math.factorial
    sides = [
        2.0 * (-1.0) ** (k + 1) * fact(6) ** 2 / (k * k * fact(6 - k) * fact(6 + k))
        for k in range(1, 7)
    ]
    return (-2.0 * sum(sides), sides)


CENTER, SIDES = stencil_weights()
SCALE = -0.5 * (1.0 / 0.36)


def side_table(distance):
    table = np.zeros(distance.shape, np.float64)
    for step in range(1, REACH + 1):
        table += np.where(np.abs(distance) == step, SCALE * SIDES[step - 1], 0.0)
    return table


def halves(table):
    high = table.astype(ml_dtypes.bfloat16)
    low = (table - high.astype(np.float64)).astype(ml_dtypes.bfloat16)
    return np.stack([high, low])


def plane_matrix():
    k = np.arange(LANES + 2 * EDGE)[:, None] - EDGE
    n = np.arange(LANES)[None, :]
    dy = k // NZ - n // NZ
    dz = k % NZ - n % NZ
    return halves(np.where(dz == 0, side_table(dy), 0.0) + np.where(dy == 0, side_table(dz), 0.0))


def packed_rows(each, planes):
    r = np.arange(2 * each * planes)
    half, inner = r // (each * planes), r % (each * planes)
    return half, inner // each, inner % each


def cross_matrices(each, planes):
    half, plane, slot = packed_rows(each, planes)
    here = half * planes + plane
    edge = np.where(half == 0, plane - planes, plane + 2 * planes)
    same = slot[:, None] == slot[None, :]
    mid = np.where(same, side_table(here[:, None] - here[None, :]), 0.0)
    out = np.where(same, side_table(here[:, None] - edge[None, :]), 0.0)
    return np.stack([halves(mid), halves(out)])


def spread_matrix(each, planes, tall):
    half, plane, slot = packed_rows(each, planes)
    return ((half * tall + plane)[:, None] == np.arange(2 * tall)[None, :]).astype(np.float32)


def order_matrix(each, planes):
    group, plane, slot = packed_rows(each, planes)
    natural = plane * 2 * each + group * each + slot
    return (natural[:, None] == np.arange(natural.size)[None, :]).astype(ml_dtypes.bfloat16)


def split(value):
    high = value.astype(jnp.bfloat16)
    return high, (value - high.astype(jnp.float32)).astype(jnp.bfloat16)


def dot3(left_high, left_low, right_high, right_low):
    dot = functools.partial(jnp.dot, preferred_element_type=jnp.float32)
    return dot(left_high, right_high) + (dot(left_high, right_low) + dot(left_low, right_high))


def reorder(order, value):
    high = value.astype(jnp.bfloat16)
    rest = value - high.astype(jnp.float32)
    middle = rest.astype(jnp.bfloat16)
    low = (rest - middle.astype(jnp.float32)).astype(jnp.bfloat16)
    dot = functools.partial(jnp.dot, preferred_element_type=jnp.float32)
    return dot(order, high) + (dot(order, middle) + dot(order, low))


def filter_kernel(
    dom_size, band_size, states, potential, live, spread, near, cross, pack, unpack,
    natural, own_filtered, own_image, every,
    fields, given, halo, held, field, shared, gone,
    halo_send, halo_recv, pair_send, pair_recv, pot_sem, core_send, core_recv, far_send, far_recv, on_send, on_recv, own_sem,
):
    cells = states.shape[1]
    chunks = cells // LANES
    rows = states.shape[0]
    block = rows // 2
    dom, band = lax.axis_index("dom"), lax.axis_index("band")
    member = lax.rem(dom, 2)
    partner = dom + 1 - 2 * member
    core = lax.rem(band, 2)
    twin = band + 1 - 2 * core
    place = band // 2
    places = band_size // 2
    has_low, has_high = dom >= 2, dom < dom_size - 2
    far = [2 * lax.rem(place + step, places) + core for step in range(1, places)]
    back = [2 * lax.rem(place + places - step, places) + core for step in range(1, places)]
    whom = lambda **at: dict(device_id=at, device_id_type=pl.DeviceIdType.MESH)

    barrier = pltpu.get_barrier_semaphore()
    pl.semaphore_signal(barrier, inc=1, **whom(dom=partner))
    pl.semaphore_signal(barrier, inc=1, **whom(band=twin))
    for other in far:
        pl.semaphore_signal(barrier, inc=1, **whom(band=other))

    @pl.when(has_low)
    def _():
        pl.semaphore_signal(barrier, inc=1, **whom(dom=dom - 2))

    @pl.when(has_high)
    def _():
        pl.semaphore_signal(barrier, inc=1, **whom(dom=dom + 2))

    pl.semaphore_wait(barrier, 1 + places + has_low.astype(jnp.int32) + has_high.astype(jnp.int32))

    def lanes(c, edge=0, width=LANES):
        return pl.ds(pl.multiple_of(c * LANES + edge, 128), width)

    def remote(source, target, send, recv, **at):
        return pltpu.make_async_remote_copy(source, target, send, recv, **whom(**at))

    def pot_copy():
        return remote(potential, shared.at[member], pot_sem.at[0], pot_sem.at[1], dom=partner)

    def pair_copy(step, c):
        at = lanes(c)
        source = (given, fields.at[3, 1 - member], gone)[step]
        target = (fields.at[0, member], own_filtered.at[member], own_image.at[member])[step]
        return remote(source.at[:, at], target.at[:, at], pair_send.at[step, c], pair_recv.at[step, c], dom=partner)

    def halo_copy(k, side, c, to=None):
        at = lanes(c)
        to = dom + 4 * side - 2 if to is None else to
        return remote(
            fields.at[k, side, :, at], halo.at[k, 1 - side, :, at],
            halo_send.at[k, side, c], halo_recv.at[k, 1 - side, c], dom=to,
        )

    def at_side(side, act):
        pl.when(has_low if side == 0 else has_high)(act)

    def send_halo(k, side, c):
        at_side(side, lambda: halo_copy(k, side, c).start())

    def core_copy(c):
        at = lanes(c)
        return [
            remote(own_filtered.at[g, :, at], every.at[band, g, :, at], core_send.at[g, c], core_recv.at[g, c], band=twin)
            for g in range(2)
        ]

    def far_copy(step, c):
        at = lanes(c)
        return [
            remote(
                own_filtered.at[g, :, at], every.at[band, g, :, at],
                far_send.at[step, g, c], far_recv.at[step, g, c], band=far[step],
            )
            for g in range(2)
        ]

    def on_copy(step, c):
        at = lanes(c)
        return [
            remote(
                every.at[back[step], g, :, at], every.at[back[step], g, :, at],
                on_send.at[step, g, c], on_recv.at[step, g, c], band=twin,
            )
            for g in range(2)
        ]

    def own_copy(c):
        at = lanes(c)
        return [
            pltpu.make_async_copy(own_filtered.at[g, :, at], every.at[band, g, :, at], own_sem.at[g, c])
            for g in range(2)
        ]

    def keep(part, c, value):
        at = lanes(c, EDGE)
        high, low = split(value)
        held[part, 0, :, at] = high
        held[part, 1, :, at] = low

    pot_copy().start()
    shared[member] = potential[...]
    for part in range(2):
        for half in range(2):
            held[part, half, :, 0:EDGE] = jnp.zeros((rows, EDGE), jnp.bfloat16)
            held[part, half, :, EDGE + cells :] = jnp.zeros((rows, EDGE), jnp.bfloat16)

    @pl.loop(0, chunks)
    def _(c):
        at = lanes(c)
        packed = reorder(pack[...], states[:, at]) * live[...]
        first, second = packed[:block], packed[block:]
        fields[0, member, :, at] = jnp.where(member == 0, first, second)
        given[:, at] = jnp.where(member == 0, second, first)
        pair_copy(0, c).start()
        for side in range(2):
            pl.when(member == side)(lambda side=side: send_halo(0, side, c))

        @pl.when(jnp.logical_not(has_low))
        def _():
            for k in range(4):
                halo[k, 0, :, at] = jnp.zeros((block, LANES), jnp.float32)

        @pl.when(jnp.logical_not(has_high))
        def _():
            for k in range(4):
                halo[k, 1, :, at] = jnp.zeros((block, LANES), jnp.float32)

    pot_copy().wait()

    def arrive(c):
        at = lanes(c)
        pair_copy(0, c).wait_recv()
        for side in range(2):
            pl.when(member == 1 - side)(lambda side=side: send_halo(0, side, c))
        keep(0, c, jnp.concatenate([fields[0, 0, :, at], fields[0, 1, :, at]], axis=0))
        pots = jnp.concatenate([shared[0, :, at], shared[1, :, at]], axis=0)
        field[:, at] = jnp.dot(
            spread[...], pots, precision=lax.Precision.HIGHEST, preferred_element_type=jnp.float32
        ) + 3.0 * CENTER * SCALE

    def gather(c):
        at = lanes(c)
        pair_copy(1, c).wait_recv()
        for step in range(places - 1):
            for copy in far_copy(step, c):
                copy.start()
        for copy in core_copy(c) + own_copy(c):
            copy.start()
        both = jnp.concatenate([own_filtered[0, :, at], own_filtered[1, :, at]], axis=0)
        natural[:, at] = reorder(unpack[...], both)

    def forward(c):
        for step in range(places - 1):
            for copy in far_copy(step, c):
                copy.wait_recv()
            for copy in on_copy(step, c):
                copy.start()

    def apply(k, c, gain, own):
        at = lanes(c)
        part = k % 2
        for side in range(2):
            at_side(side, lambda side=side: halo_copy(k, 1 - side, c, partner).wait_recv())
        wide, mid = lanes(c, 0, LANES + 2 * EDGE), lanes(c, EDGE)
        total = dot3(held[part, 0, :, wide], held[part, 1, :, wide], near[0], near[1])
        total += dot3(cross[0, 0], cross[0, 1], held[part, 0, :, mid], held[part, 1, :, mid])
        out_high, out_low = split(jnp.concatenate([halo[k, 0, :, at], halo[k, 1, :, at]], axis=0))
        total += dot3(cross[1, 0], cross[1, 1], out_high, out_low)
        value = jnp.concatenate([fields[k, 0, :, at], fields[k, 1, :, at]], axis=0)
        result = gain * (field[:, at] * value + total) + own * value
        if k in (1, 2):
            result = result - jnp.concatenate([fields[k - 1, 0, :, at], fields[k - 1, 1, :, at]], axis=0)
        if k < 3:
            fields[k + 1, 0, :, at] = result[:block]
            fields[k + 1, 1, :, at] = result[block:]
            for side in range(2):
                send_halo(k + 1, side, c)
            keep(1 - part, c, result)
        return result

    for c in range(2):
        arrive(c)

    @pl.loop(0, chunks)
    def _(c):
        pl.when(c + 2 < chunks)(lambda: arrive(c + 2))
        apply(0, c, 1.0 / 11.0, -1.0)

    @pl.loop(0, chunks)
    def _(c):
        apply(1, c, 2.0 / 11.0, -2.0)

    @pl.loop(0, chunks)
    def _(c):
        at = lanes(c)
        result = apply(2, c, 2.0 / 11.0, -2.0)
        pair_copy(1, c).start()
        own_filtered[member, :, at] = jnp.where(member == 0, result[:block], result[block:])
        pl.when(c >= 2)(lambda: gather(c - 2))

    pl.loop(chunks - 2, chunks)(gather)
    lag = 4

    @pl.loop(0, chunks)
    def _(c):
        at = lanes(c)
        result = apply(3, c, 1.0, 0.0)
        own_image[member, :, at] = jnp.where(member == 0, result[:block], result[block:])
        gone[:, at] = jnp.where(member == 0, result[block:], result[:block])
        pair_copy(2, c).start()
        pl.when(c >= lag)(lambda: forward(c - lag))

    pl.loop(chunks - lag, chunks)(forward)

    @pl.loop(0, chunks)
    def _(c):
        pair_copy(2, c).wait_recv()
        for step in range(3):
            pair_copy(step, c).wait_send()
        for k in range(4):
            for side in range(2):
                at_side(side, lambda k=k, side=side: halo_copy(k, side, c).wait_send())
        for copy in core_copy(c):
            copy.wait()
        for copy in own_copy(c):
            copy.wait()
        for step in range(places - 1):
            for copy in far_copy(step, c):
                copy.wait_send()
            for copy in on_copy(step, c):
                copy.wait()


def run_filter(states, potential, live, each, planes, dom_size, band_size):
    rows, cells = states.shape
    block, chunks, tall = rows // 2, cells // LANES, potential.shape[0]
    order = order_matrix(each, planes)
    f32 = lambda *shape: pltpu.VMEM(shape, jnp.float32)
    dma = lambda *shape: pltpu.SemaphoreType.DMA(shape)
    out = lambda *shape: jax.ShapeDtypeStruct(shape, jnp.float32)
    others = max(band_size // 2 - 1, 1)
    vmem = pl.BlockSpec(memory_space=pltpu.VMEM)
    return pl.pallas_call(
        functools.partial(filter_kernel, dom_size, band_size),
        out_shape=(
            out(rows, cells), out(2, block, cells), out(2, block, cells), out(band_size, 2, block, cells),
        ),
        in_specs=[vmem] * 8,
        out_specs=(vmem, vmem, vmem, pl.BlockSpec(memory_space=pl.ANY)),
        scratch_shapes=[
            f32(4, 2, block, cells), f32(block, cells), f32(4, 2, block, cells),
            pltpu.VMEM((2, 2, rows, cells + 2 * EDGE), jnp.bfloat16),
            f32(rows, cells), f32(2, tall, cells), f32(block, cells),
            dma(4, 2, chunks), dma(4, 2, chunks), dma(3, chunks), dma(3, chunks), dma(2),
            dma(2, chunks), dma(2, chunks), dma(others, 2, chunks), dma(others, 2, chunks),
            dma(others, 2, chunks), dma(others, 2, chunks), dma(2, chunks),
        ],
        compiler_params=pltpu.CompilerParams(
            vmem_limit_bytes=VMEM_BYTES, collective_id=0, has_side_effects=True
        ),
        name="filter_states",
    )(
        states, potential, live, jnp.asarray(spread_matrix(each, planes, tall)), jnp.asarray(plane_matrix()),
        jnp.asarray(cross_matrices(each, planes)), jnp.asarray(order), jnp.asarray(order.T),
    )


def gram_kernel(own, image, every, same, fold_left, fold_right, out, total):
    step = pl.program_id(0)

    @pl.when(step == 0)
    def _():
        total[...] = jnp.zeros_like(total)

    every_high, every_low = split(every[...])
    dot = functools.partial(
        lax.dot_general, dimension_numbers=(((1,), (1,)), ((), ())), preferred_element_type=jnp.float32
    )
    for which, ref in enumerate((own, image)):
        high, low = split(ref[...])
        total[which] += dot(high, every_high) + (dot(high, every_low) + dot(low, every_high))

    @pl.when(step == pl.num_programs(0) - 1)
    def _():
        exact = functools.partial(
            jnp.dot, precision=lax.Precision.HIGHEST, preferred_element_type=jnp.float32
        )
        for which in range(2):
            out[which] = exact(exact(fold_left[...], total[which] * same[...]), fold_right[...])


def run_gram(own, image, every, each, planes, capacity, bands):
    total, cells = own.shape
    width = every.shape[0]
    group, plane, slot = packed_rows(each, planes)
    index = group * each + slot
    fold = (index[None, :] == np.arange(capacity)[:, None]).astype(np.float32)
    same = (plane[:, None] == np.tile(plane, bands)[None, :]).astype(np.float32)
    fold_right = np.kron(np.eye(bands, dtype=np.float32), fold.T)
    block = pl.BlockSpec((total, LANES), lambda i: (0, i))
    return pl.pallas_call(
        gram_kernel,
        grid=(cells // LANES,),
        out_shape=jax.ShapeDtypeStruct((2, capacity, bands * capacity), jnp.float32),
        in_specs=[
            block,
            block,
            pl.BlockSpec((width, LANES), lambda i: (0, i)),
            pl.BlockSpec(memory_space=pltpu.VMEM),
            pl.BlockSpec(memory_space=pltpu.VMEM),
            pl.BlockSpec(memory_space=pltpu.VMEM),
        ],
        out_specs=pl.BlockSpec((2, capacity, bands * capacity), lambda i: (0, 0, 0)),
        scratch_shapes=[pltpu.VMEM((2, total, width), jnp.float32)],
        compiler_params=pltpu.CompilerParams(vmem_limit_bytes=VMEM_BYTES),
        name="gram",
    )(own, image, every, jnp.asarray(same), jnp.asarray(fold), jnp.asarray(fold_right))


def local(states, potential, counts):
    capacity, planes, cells = states.shape
    dom_size, bands = lax.axis_size("dom"), lax.axis_size("band")
    each = capacity // 2
    rows = capacity * planes
    live_count = counts[lax.axis_index("band")]
    group, plane, slot = packed_rows(each, planes)
    live = (jnp.asarray(group * each + slot, jnp.int32) < live_count).astype(jnp.float32)[:, None]
    tall_potential = jnp.pad(potential, ((0, -planes % 8), (0, 0)))
    natural, filtered, image, every = run_filter(
        states.transpose(1, 0, 2).reshape(rows, cells), tall_potential, live, each, planes, dom_size, bands
    )
    terms = run_gram(
        filtered.reshape(rows, cells), image.reshape(rows, cells), every.reshape(bands * rows, cells),
        each, planes, capacity, bands,
    )
    projected = lax.psum_scatter(terms, "dom", scatter_dimension=2, tiled=True)
    return natural.reshape(planes, capacity, cells).transpose(1, 0, 2), projected


def solution(mesh):
    return jax.shard_map(
        local,
        mesh=mesh,
        in_specs=(P("band", "dom", None), P("dom", None), P()),
        out_specs=(P("band", "dom", None), P(None, "band", "dom")),
        check_vma=False,
    )
```

time: 434 us -> 255 us (0.59)
  blocking collectives: 226 us -> 38.1 us
  Pallas kernels: 72.1 us -> 204 us
  waiting for transfers between devices: 75.3 us -> 0 us
  local copies, waits for them, and re-layouts: 29.7 us -> 9.77 us
  between operations: 14.8 us -> 1.33 us
  starting transfers between devices: 12.1 us -> 0 us
    pallas_call x1, Pallas kernels: 50.1 us -> 181 us  [run_filter(): pl.pallas_call(functools.partial(filter_kernel, dom_size, band_size), out...]
    all_gather x1 -> x0, blocking collectives: 104 us -> none  [local(): whole_potential = lax.all_gather(potential, 'dom', axis=0, tiled=True)]
    all_to_all x1 -> x0, blocking collectives: 83.1 us -> none  [local(): lax.all_to_all(a.reshape(parts, rows, cells), 'dom', 0, 0, tiled=True)]
    all_to_all x2 -> x0, waiting for transfers between devices: 66.8 us -> none  [the longest x1 66.8 us: local(): lax.all_to_all(a.reshape(parts, rows, cells), 'dom', 0, 0, tiled=True)]
    all_to_all x2 -> x0, starting transfers between devices: 12.1 us -> none  [the longest x1 7.38 us: local(): lax.all_to_all(start, 'dom', 0, 0, tiled=True).reshape(parts * rows, cells)]
    reshape x2 -> x0, local copies, waits for them, and re-layouts: 9.91 us -> none  [the longest x1 5.01 us: local(): result = result.reshape(parts * each, planes, cells)[:capacity]]
    all_gather x1 -> x0, waiting for transfers between devices: 8.52 us -> none  [local(): every = lax.all_gather(filtered, 'band', axis=0, tiled=True)]
    unnamed x8 -> x5, local copies, waits for them, and re-layouts: 9.1 us -> 5.18 us
  transfers between devices with their start and end apart: 3 -> 0, of which waited for: 2 -> 0; matrix products, arithmetic and copies ran while one was open for 3% -> 0% of each run, Pallas kernels for 0% -> 0%
where the time goes in v2:
time: 255 us; the launch traced here: 254 us
  Pallas kernels  204 us (80%)
  blocking collectives  38.1 us (15%)
  local copies, waits for them, and re-layouts  9.77 us (4%)
    pallas_call x1, Pallas kernels, run_filter(): pl.pallas_call(functools.partial(filter_kernel, dom_size, band_size), out...  181 us
    unnamed x1, blocking collectives  38.1 us
    pallas_call x1, Pallas kernels, run_gram(): pl.pallas_call(gram_kernel, grid=(cells // LANES,), out_shape=jax.ShapeDt...  22.2 us
    unnamed x5, local copies, waits for them, and re-layouts  5.18 us

profile of v2, /device:TPU:0, one launch (start us, length us, event | category | flops | bytes accessed | tf_op | source)
XLA Modules:
  0.0 254.0 jit_solution(5504089283404409013)
XLA Ops:
  0.6 1.2 dynamic_slice.3
  1.9 1.3 compare_convert_fusion
  3.2 0.8 copy.17.live
  4.0 1.6 pad.4.potential
  5.6 181.4 %filter_states.1 = (f32[240,3584]{1,0:T(8,128)}, f32[2,120,3584]{2,1,0:T(8,128)}, f32[2,120,3584]{2,1,0:T(8,128)}, f32[4,2,120,3584]{3,2,1,0:T(8,128)}) custom-call(f32[240,3584]{1,0:T(8,128)} %bitcast.13, f32[8,3584]{1,0:T(8,128)} %pad.4.potential, f32[240,1]{1,0:T(8,128)} %copy.17.live, f32[240,16]{1,0:T(8,128)} %constant.29.clone.spread, ...), custom_call_target="tpu_custom_call" | custom-call | tf_op jit(solution)/shard_map/filter_states/pallas_call | solution.py:351
  186.9 0.0 copy-start
  187.0 22.2 %gram.1 = f32[2,40,160]{2,1,0:T(8,128)} custom-call(f32[240,3584]{1,0:T(8,128)} %bitcast.15, f32[240,3584]{1,0:T(8,128)} %bitcast.16, f32[960,3584]{1,0:T(8,128)} %bitcast.12, f32[240,960]{1,0:T(8,128)} %constant.34.clone.same, f32[40,240]{1,0:T(8,128)} %constant.35.clone.fold_left, f32[960,160]{1,0:T(8,128)} %constant.36.clone.fold_right), custom_call_target="tpu_custom_call" | custom-call | tf_op jit(solution)/shard_map/gram/pallas_call | solution.py:409
  209.1 1.0 copy.18
  210.1 38.1 %all-reduce.1 = f32[2,40,160]{1,0,2:T(2,128)S(1)} all-reduce(f32[2,40,160]{1,0,2:T(2,128)S(1)} %copy.18), channel_id=2, replica_groups=mesh['dom'=8,'band'=4] {'dom'}, use_global_device_ids=true, to_apply=%region_0.1.clone | all-reduce | flops 12800 | bytes 102400
  248.2 0.0 copy-done
  248.2 0.6 dynamic-slice
  249.4 0.6 constant_dynamic-slice_fusion
  250.1 4.0 %copy.20 = f32[40,6,3584]{2,0,1:T(8,128)} copy(f32[40,6,3584]{2,0,1:T(8,128)} %bitcast.14) | data formatting | bytes 6881280
Async XLA Ops:
  186.9 61.3 %copy-start = (u32[32]{0:T(128)S(1)}, u32[32]{0:T(128)}, u32[]{:S(2)}) copy-start(u32[32]{0:T(128)} %constant.43) | copy-start | bytes 388

commit v3 on v2

--- a/solution.py
+++ b/solution.py
@@ -220,8 +220,6 @@
         fields[0, member, :, at] = jnp.where(member == 0, first, second)
         given[:, at] = jnp.where(member == 0, second, first)
         pair_copy(0, c).start()
-        for side in range(2):
-            pl.when(member == side)(lambda side=side: send_halo(0, side, c))
 
         @pl.when(jnp.logical_not(has_low))
         def _():
@@ -239,7 +237,7 @@
         at = lanes(c)
         pair_copy(0, c).wait_recv()
         for side in range(2):
-            pl.when(member == 1 - side)(lambda side=side: send_halo(0, side, c))
+            send_halo(0, side, c)
         keep(0, c, jnp.concatenate([fields[0, 0, :, at], fields[0, 1, :, at]], axis=0))
         pots = jnp.concatenate([shared[0, :, at], shared[1, :, at]], axis=0)
         field[:, at] = jnp.dot(
@@ -286,39 +284,39 @@
             keep(1 - part, c, result)
         return result
 
-    for c in range(2):
-        arrive(c)
-
-    @pl.loop(0, chunks)
-    def _(c):
-        pl.when(c + 2 < chunks)(lambda: arrive(c + 2))
-        apply(0, c, 1.0 / 11.0, -1.0)
-
-    @pl.loop(0, chunks)
-    def _(c):
-        apply(1, c, 2.0 / 11.0, -2.0)
-
-    @pl.loop(0, chunks)
-    def _(c):
-        at = lanes(c)
+    def third(c):
         result = apply(2, c, 2.0 / 11.0, -2.0)
+        own_filtered[member, :, lanes(c)] = jnp.where(member == 0, result[:block], result[block:])
         pair_copy(1, c).start()
-        own_filtered[member, :, at] = jnp.where(member == 0, result[:block], result[block:])
-        pl.when(c >= 2)(lambda: gather(c - 2))
-
-    pl.loop(chunks - 2, chunks)(gather)
-    lag = 4
-
-    @pl.loop(0, chunks)
-    def _(c):
+
+    def fourth(c):
         at = lanes(c)
         result = apply(3, c, 1.0, 0.0)
         own_image[member, :, at] = jnp.where(member == 0, result[:block], result[block:])
         gone[:, at] = jnp.where(member == 0, result[block:], result[:block])
         pair_copy(2, c).start()
-        pl.when(c >= lag)(lambda: forward(c - lag))
-
-    pl.loop(chunks - lag, chunks)(forward)
+
+    for c in range(2):
+        arrive(c)
+
+    stages = (
+        (-2, arrive),
+        (0, lambda c: apply(0, c, 1.0 / 11.0, -1.0)),
+        (3, lambda c: apply(1, c, 2.0 / 11.0, -2.0)),
+        (6, third),
+        (9, fourth),
+        (7, gather),
+        (8, forward),
+    )
+
+    @pl.loop(0, chunks + 9)
+    def _(wave):
+        for behind, stage in stages:
+            c = wave - behind
+
+            @pl.when((c >= 0) & (c < chunks))
+            def _(c=c, stage=stage):
+                stage(c)
 
     @pl.loop(0, chunks)
     def _(c):
@@ -373,31 +371,60 @@
     )
 
 
-def gram_kernel(own, image, every, same, fold_left, fold_right, out, total):
+def gram_kernel(dom_size, own, image, every, same, fold_left, fold_right, pick, out, total, mine, theirs, send, recv):
     step = pl.program_id(0)
+    rows = own.shape[0]
+    dom = lax.axis_index("dom")
+    barrier = pltpu.get_barrier_semaphore()
 
     @pl.when(step == 0)
     def _():
         total[...] = jnp.zeros_like(total)
+        for shift in range(1, dom_size):
+            pl.semaphore_signal(
+                barrier, inc=1, device_id=dict(dom=lax.rem(dom + shift, dom_size)), device_id_type=pl.DeviceIdType.MESH
+            )
 
     every_high, every_low = split(every[...])
-    dot = functools.partial(
-        lax.dot_general, dimension_numbers=(((1,), (1,)), ((), ())), preferred_element_type=jnp.float32
-    )
-    for which, ref in enumerate((own, image)):
-        high, low = split(ref[...])
-        total[which] += dot(high, every_high) + (dot(high, every_low) + dot(low, every_high))
+    high, low = split(jnp.concatenate([own[...], image[...]], axis=0))
+    total[...] += lax.dot_general(
+        jnp.concatenate([high, high, low], axis=1),
+        jnp.concatenate([every_high, every_low, every_high], axis=1),
+        (((1,), (1,)), ((), ())),
+        preferred_element_type=jnp.float32,
+    )
 
     @pl.when(step == pl.num_programs(0) - 1)
     def _():
         exact = functools.partial(
             jnp.dot, precision=lax.Precision.HIGHEST, preferred_element_type=jnp.float32
         )
+        terms = [
+            exact(exact(fold_left[...], total[which * rows : (which + 1) * rows] * same[...]), fold_right[...])
+            for which in range(2)
+        ]
+        pl.semaphore_wait(barrier, dom_size - 1)
+        copies = []
+        for shift in range(1, dom_size):
+            to = lax.rem(dom + shift, dom_size)
+            for which in range(2):
+                mine[shift, which] = exact(terms[which], pick[to])
+            copy = pltpu.make_async_remote_copy(
+                mine.at[shift], theirs.at[shift], send.at[shift], recv.at[shift],
+                device_id=dict(dom=to), device_id_type=pl.DeviceIdType.MESH,
+            )
+            copy.start()
+            copies.append(copy)
+        sums = [exact(terms[which], pick[dom]) for which in range(2)]
+        for shift, copy in enumerate(copies, 1):
+            copy.wait()
+            for which in range(2):
+                sums[which] = sums[which] + theirs[shift, which]
         for which in range(2):
-            out[which] = exact(exact(fold_left[...], total[which] * same[...]), fold_right[...])
-
-
-def run_gram(own, image, every, each, planes, capacity, bands):
+            out[which] = sums[which][:, : out.shape[2]]
+
+
+def run_gram(own, image, every, each, planes, capacity, bands, dom_size):
     total, cells = own.shape
     width = every.shape[0]
     group, plane, slot = packed_rows(each, planes)
@@ -405,24 +432,28 @@
     fold = (index[None, :] == np.arange(capacity)[:, None]).astype(np.float32)
     same = (plane[:, None] == np.tile(plane, bands)[None, :]).astype(np.float32)
     fold_right = np.kron(np.eye(bands, dtype=np.float32), fold.T)
-    block = pl.BlockSpec((total, LANES), lambda i: (0, i))
+    columns = bands * capacity // dom_size
+    lane = np.arange(-(-columns // 128) * 128)
+    at = np.arange(dom_size)[:, None, None] * columns + lane[None, None, :]
+    pick = ((np.arange(bands * capacity)[None, :, None] == at) & (lane < columns)).astype(np.float32)
+    block = pl.BlockSpec((total, 2 * LANES), lambda i: (0, i))
+    whole = pl.BlockSpec(memory_space=pltpu.VMEM)
+    parcel = pltpu.VMEM((dom_size, 2, capacity, lane.size), jnp.float32)
     return pl.pallas_call(
-        gram_kernel,
-        grid=(cells // LANES,),
-        out_shape=jax.ShapeDtypeStruct((2, capacity, bands * capacity), jnp.float32),
-        in_specs=[
-            block,
-            block,
-            pl.BlockSpec((width, LANES), lambda i: (0, i)),
-            pl.BlockSpec(memory_space=pltpu.VMEM),
-            pl.BlockSpec(memory_space=pltpu.VMEM),
-            pl.BlockSpec(memory_space=pltpu.VMEM),
+        functools.partial(gram_kernel, dom_size),
+        grid=(cells // (2 * LANES),),
+        out_shape=jax.ShapeDtypeStruct((2, capacity, columns), jnp.float32),
+        in_specs=[block, block, pl.BlockSpec((width, 2 * LANES), lambda i: (0, i)), whole, whole, whole, whole],
+        out_specs=pl.BlockSpec((2, capacity, columns), lambda i: (0, 0, 0)),
+        scratch_shapes=[
+            pltpu.VMEM((2 * total, width), jnp.float32), parcel, parcel,
+            pltpu.SemaphoreType.DMA((dom_size,)), pltpu.SemaphoreType.DMA((dom_size,)),
         ],
-        out_specs=pl.BlockSpec((2, capacity, bands * capacity), lambda i: (0, 0, 0)),
-        scratch_shapes=[pltpu.VMEM((2, total, width), jnp.float32)],
-        compiler_params=pltpu.CompilerParams(vmem_limit_bytes=VMEM_BYTES),
+        compiler_params=pltpu.CompilerParams(
+            vmem_limit_bytes=VMEM_BYTES, collective_id=1, has_side_effects=True
+        ),
         name="gram",
-    )(own, image, every, jnp.asarray(same), jnp.asarray(fold), jnp.asarray(fold_right))
+    )(own, image, every, jnp.asarray(same), jnp.asarray(fold), jnp.asarray(fold_right), jnp.asarray(pick))
 
 
 def local(states, potential, counts):
@@ -437,11 +468,10 @@
     natural, filtered, image, every = run_filter(
         states.transpose(1, 0, 2).reshape(rows, cells), tall_potential, live, each, planes, dom_size, bands
     )
-    terms = run_gram(
+    projected = run_gram(
         filtered.reshape(rows, cells), image.reshape(rows, cells), every.reshape(bands * rows, cells),
-        each, planes, capacity, bands,
-    )
-    projected = lax.psum_scatter(terms, "dom", scatter_dimension=2, tiled=True)
+        each, planes, capacity, bands, dom_size,
+    )
     return natural.reshape(planes, capacity, cells).transpose(1, 0, 2), projected
 
 

time: 255 us -> 219 us (0.86)
  blocking collectives: 38.1 us -> 0 us
  Pallas kernels: 204 us -> 207 us
    unnamed x1 -> x0, blocking collectives: 38.1 us -> none
    pallas_call x1, Pallas kernels: 22.2 us -> 26.5 us  [run_gram(): pl.pallas_call(functools.partial(gram_kernel, dom_size), grid=(cells // (...]
    unnamed x5 -> x2, local copies, waits for them, and re-layouts: 5.18 us -> 5.45 us
where the time goes in v3:
time: 219 us; the launch traced here: 218 us
  Pallas kernels  207 us (95%)
  local copies, waits for them, and re-layouts  9.03 us (4%)
    pallas_call x1, Pallas kernels, run_filter(): pl.pallas_call(functools.partial(filter_kernel, dom_size, band_size), out...  181 us
    pallas_call x1, Pallas kernels, run_gram(): pl.pallas_call(functools.partial(gram_kernel, dom_size), grid=(cells // (...  26.5 us
    unnamed x2, local copies, waits for them, and re-layouts  5.45 us

profile of v3, /device:TPU:0, one launch (start us, length us, event | category | flops | bytes accessed | tf_op | source)
XLA Modules:
  0.0 218.4 jit_solution(4710817985630391131)
XLA Ops:
  0.6 1.2 dynamic_slice.3
  1.9 1.3 compare_convert_fusion
  3.2 0.8 copy.16.live
  4.0 1.6 pad.4.potential
  5.5 180.9 %filter_states.1 = (f32[240,3584]{1,0:T(8,128)}, f32[2,120,3584]{2,1,0:T(8,128)}, f32[2,120,3584]{2,1,0:T(8,128)}, f32[4,2,120,3584]{3,2,1,0:T(8,128)}) custom-call(f32[240,3584]{1,0:T(8,128)} %bitcast.14, f32[8,3584]{1,0:T(8,128)} %pad.4.potential, f32[240,1]{1,0:T(8,128)} %copy.16.live, f32[240,16]{1,0:T(8,128)} %constant.31.clone.spread, ...), custom_call_target="tpu_custom_call" | custom-call | tf_op jit(solution)/shard_map/filter_states/pallas_call | solution.py:349
  186.5 26.5 %gram.1 = f32[2,40,20]{2,1,0:T(8,128)} custom-call(f32[240,3584]{1,0:T(8,128)} %bitcast.12, f32[240,3584]{1,0:T(8,128)} %bitcast.13, f32[960,3584]{1,0:T(8,128)} %bitcast.11, f32[240,960]{1,0:T(8,128)} %constant.36.clone.same, f32[40,240]{1,0:T(8,128)} %constant.37.clone.fold_left, f32[960,160]{1,0:T(8,128)} %constant.38.clone.fold_right, ...), custom_call_target="tpu_custom_call" | custom-call | tf_op jit(solution)/shard_map/gram/pallas_call | solution.py:442
  212.9 1.5 copy.17
  214.4 4.0 %copy.19 = f32[40,6,3584]{2,0,1:T(8,128)} copy(f32[40,6,3584]{2,0,1:T(8,128)} %bitcast.15) | data formatting | bytes 6881280
